TPU v7x, 32 devices: a whole 2x2x4 slice. The times are simulated.
32 devices in a mesh: dp: 8 (over y, x, core), tensor: 4 (over z).
Axes of the slice: x: 2, y: 2, z: 4, core: 2. Of those that a mesh axis runs over, the one named last changes fastest.
Arguments:
- inputs: bfloat16 [4096, 6144], P(('dp', 'tensor')), may hold values from -36 to 36
- gain: float32 [6144], replicated, may hold values from 0.25 to 1.75
- w_in: bfloat16 [6144, 12288], P(None, 'tensor'), may hold values from -0.078125 to 0.078125
- grad_act: bfloat16 [4096, 12288], P('dp', 'tensor'), may hold values from -6 to 6
- residual_gradient: bfloat16 [4096, 6144], P(('dp', 'tensor')), may hold values from -6 to 6
Outputs:
- block_input_gradient: bfloat16 [4096, 6144], P(('dp', 'tensor'))
- grad_w: float32 [6144, 12288], P('dp', 'tensor')
- scale_gradient: float32 [6144], replicated
All inputs are finite; a program needn't handle non-finite values.
Results may differ from a plain program's by a relative error of at most 0.022.
Values may be sent and summed in bfloat16 or wider, within the bound.
A program may use at most 192 MiB of HBM per device.

v0:
```python
import jax
import jax.numpy as jnp
from jax import lax
from jax.sharding import PartitionSpec as P


def contract_rows(left, right):
    return lax.dot_general(
        left, right, (((0,), (0,)), ((), ())), preferred_element_type=jnp.float32
    )


def on_device(inputs, gain, w_in, grad_act, residual_gradient):
    values = inputs.astype(jnp.float32)
    centered_input = values - jnp.mean(values, axis=1, keepdims=True)
    inverse_deviation = lax.rsqrt(
        jnp.mean(centered_input * centered_input, axis=1, keepdims=True) + 1e-06
    )
    standardized_input = centered_input * inverse_deviation
    normed_output = (standardized_input * gain).astype(jnp.bfloat16)
    replicas = lax.axis_size("dp")
    full = lax.all_gather(normed_output, "tensor", axis=0, tiled=True)
    pre = jnp.dot(full, w_in, preferred_element_type=jnp.float32)
    unused, pullback = jax.vjp(jax.nn.gelu, pre)
    dpre = pullback(grad_act.astype(jnp.float32))[0].astype(jnp.bfloat16)
    normed_gradient = lax.psum_scatter(
        lax.dot_general(
            dpre, w_in, (((1,), (1,)), ((), ())), preferred_element_type=jnp.float32
        ).astype(jnp.bfloat16),
        "tensor",
        scatter_dimension=0,
        tiled=True,
    ).astype(jnp.float32)
    scale_terms = jnp.sum(normed_gradient * standardized_input, axis=0)
    scale_gradient = lax.psum(scale_terms, ("dp", "tensor")) / replicas
    scaled_gradient = normed_gradient * gain
    first_average = jnp.mean(scaled_gradient, axis=1, keepdims=True)
    second_average = jnp.mean(scaled_gradient * standardized_input, axis=1, keepdims=True)
    block_input_gradient = (
        residual_gradient.astype(jnp.float32)
        + inverse_deviation
        * (scaled_gradient - first_average - standardized_input * second_average)
    ).astype(jnp.bfloat16)
    term = contract_rows(full, dpre)
    grad_w = (
        lax.psum_scatter(term.astype(jnp.bfloat16), "dp", scatter_dimension=0, tiled=True).astype(
            jnp.float32
        )
        / replicas
    )
    return (block_input_gradient, grad_w, scale_gradient)


def solution(mesh):
    return jax.shard_map(
        on_device,
        mesh=mesh,
        in_specs=(
            P(("dp", "tensor"), None),
            P(),
            P(None, "tensor"),
            P("dp", "tensor"),
            P(("dp", "tensor"), None),
        ),
        out_specs=(P(("dp", "tensor"), None), P("dp", "tensor"), P()),
        check_vma=False,
    )
```

profile of v0, /device:TPU:0, one launch (start us, length us, event | category | flops | bytes accessed | tf_op | source)
XLA Modules:
  0.0 551.1 jit_solution(18289202832464980588)
XLA Ops:
  7.2 0.0 all-gather.2.cloned.1.call-start
  7.2 1.7 convert_reduce_fusion
  8.9 2.0 fusion.24
  10.9 3.1 fusion.19
  14.0 0.0 all-gather.2.cloned.1.call-update
  14.0 0.0 copy-start.3
  14.1 0.0 reduce-scatter.3.cloned.1.call-start
  14.1 118.1 %all-gather.2.cloned.1.call-done = bf16[512,6144]{1,0:T(8,128)(2,1)} async-done(((bf16[128,6144]{1,0:T(8,128)(2,1)}), bf16[512,6144]{1,0:T(8,128)(2,1)}) %all-gather.2.cloned.1.call-update) | async-done | bytes 6291472 | tf_op jit(solution)/shard_map/all_gather | solution.py:22
  132.2 26.8 %fusion.51 = f32[512,3072]{1,0:T(8,128)} fusion(bf16[512,6144]{1,0:T(8,128)(2,1)} %all-gather.2.cloned.1.call-done, bf16[6144,3072]{1,0:T(8,128)(2,1)} %param.7), kind=kOutput, calls=%fused_computation.65 | convolution fusion | flops 19327352832 | bytes 50331648 | tf_op jit(solution)/shard_map/dot_general | solution.py:23
  159.0 0.0 copy-done.3
  159.0 39.6 %convolution_convert_fusion.1 = bf16[512,6144]{1,0:T(8,128)(2,1)} fusion(bf16[6144,3072]{1,0:T(8,128)(2,1)} %param.7, bf16[512,3072]{1,0:T(8,128)(2,1)S(1)} %copy-done.3, f32[512,3072]{1,0:T(8,128)} %fusion.51), kind=kOutput, calls=%fused_computation.4 | convolution fusion | flops 19363528704 | bytes 53477376 | tf_op jit(solution)/shard_map/dot_general | solution.py:27
  198.6 0.0 reduce-scatter.3.cloned.1.call-update
  198.6 0.2 reduce-scatter.5.cloned.1.call-start
  198.8 29.0 %convolution_convert_fusion = bf16[6144,3072]{1,0:T(8,128)(2,1)} fusion(bf16[512,6144]{1,0:T(8,128)(2,1)} %all-gather.2.cloned.1.call-done, bf16[512,3072]{1,0:T(8,128)(2,1)S(1)} %copy-done.3, f32[512,3072]{1,0:T(8,128)} %fusion.51), kind=kOutput, calls=%fused_computation | convolution fusion | flops 19379257344 | bytes 53477376 | tf_op jit(solution)/shard_map/dot_general | solution.py:8
  227.9 0.0 copy-start
  227.9 0.0 copy-start.2
  227.9 0.0 copy-start.1
  227.9 0.0 reduce-scatter.5.cloned.1.call-update
  227.9 79.8 %reduce-scatter.3.cloned.1.call-done = bf16[128,6144]{1,0:T(8,128)(2,1)} async-done(((bf16[512,6144]{1,0:T(8,128)(2,1)}), bf16[128,6144]{1,0:T(8,128)(2,1)}) %reduce-scatter.3.cloned.1.call-update) | async-done | bytes 1572880 | tf_op jit(solution)/shard_map/reduce_scatter | solution.py:26
  307.7 0.0 copy-done
  307.7 0.0 copy-done.2
  307.7 2.9 fusion.26
  310.6 41.0 %psum.7 = f32[6144]{0:T(1024)S(1)} all-reduce(f32[6144]{0:T(1024)S(1)} %get-tuple-element.3), channel_id=1, replica_groups=mesh['dp'=8,'tensor'=4] {'dp','tensor'}, use_global_device_ids=true, to_apply=%region_7.0 | all-reduce | flops 6144 | bytes 49152 | tf_op jit(solution)/shard_map/psum | solution.py:35
  351.6 0.6 broadcast_multiply_fusion
  352.2 0.0 copy-done.1
  352.2 4.5 fusion.23
  356.7 180.6 %reduce-scatter.5.cloned.1.call-done = bf16[768,3072]{1,0:T(8,128)(2,1)} async-done(((bf16[6144,3072]{1,0:T(8,128)(2,1)}), bf16[768,3072]{1,0:T(8,128)(2,1)}) %reduce-scatter.5.cloned.1.call-update) | async-done | bytes 4718608 | tf_op jit(solution)/shard_map/reduce_scatter | solution.py:46
  537.3 7.3 %convert_multiply_fusion = f32[768,3072]{1,0:T(8,128)} fusion(bf16[768,3072]{1,0:T(8,128)(2,1)} %reduce-scatter.5.cloned.1.call-done), kind=kLoop, calls=%fused_computation.1 | loop fusion | flops 4718592 | bytes 14155776 | tf_op jit(solution)/shard_map/div | solution.py:46
  (3 shorter events, 0.0 us)
Async XLA Ops:
  7.2 125.1 %all-gather.2.cloned.1.call-start = ((), (), s32[]{:S(2)}) async-start(), calls=%async_computation.2 | async-start | bytes 7864320 | tf_op jit(solution)/shard_map/all_gather | solution.py:22
  14.0 145.0 %copy-start.3 = (bf16[512,3072]{1,0:T(8,128)(2,1)S(1)}, bf16[512,3072]{1,0:T(8,128)(2,1)}, u32[]{:S(2)}) copy-start(bf16[512,3072]{1,0:T(8,128)(2,1)} %param.8) | copy-start | bytes 9437188
  14.1 293.7 %reduce-scatter.3.cloned.1.call-start = ((), (), s32[]{:S(2)}) async-start(), calls=%async_computation.3 | async-start | bytes 7864320 | tf_op jit(solution)/shard_map/reduce_scatter | solution.py:26
  198.6 338.7 %reduce-scatter.5.cloned.1.call-start = ((), (), s32[]{:S(2)}) async-start(), calls=%async_computation.4 | async-start | bytes 42467328 | tf_op jit(solution)/shard_map/reduce_scatter | solution.py:46
  227.9 79.9 %copy-start = (bf16[128,6144]{1,0:T(8,128)(2,1)S(1)}, bf16[128,6144]{1,0:T(8,128)(2,1)}, u32[]{:S(2)}) copy-start(bf16[128,6144]{1,0:T(8,128)(2,1)} %param.5) | copy-start | bytes 4718596
  227.9 79.9 %copy-start.2 = (f32[6144]{0:T(1024)S(1)}, f32[6144]{0:T(1024)}, u32[]{:S(2)}) copy-start(f32[6144]{0:T(1024)} %param.6) | copy-start | bytes 73732
  227.9 124.3 %copy-start.1 = (bf16[128,6144]{1,0:T(8,128)(2,1)S(1)}, bf16[128,6144]{1,0:T(8,128)(2,1)}, u32[]{:S(2)}) copy-start(bf16[128,6144]{1,0:T(8,128)(2,1)} %param.9) | copy-start | bytes 4718596
Sparse Core Ops, SparseCore 0:
  14.2 118.0 all-gather.1
  198.7 108.9 reduce-scatter.2
  311.4 225.8 reduce-scatter.4
where the time goes:
time: 551 us
  waiting for transfers between devices  379 us (69%)
  matrix products  95.4 us (17%)
  blocking collectives  41 us (7%)
  other arithmetic  22.1 us (4%)
  between operations  13.8 us (3%)
    reduce_scatter x1, waiting for transfers between devices, on_device(): lax.psum_scatter(term.astype(jnp.bfloat16), 'dp', scatter_dimension=0, ti...  181 us
    all_gather x1, waiting for transfers between devices, on_device(): full = lax.all_gather(normed_output, 'tensor', axis=0, tiled=True)  118 us
    reduce_scatter x1, waiting for transfers between devices, on_device(): lax.psum_scatter(lax.dot_general(dpre, w_in, (((1,), (1,)), ((), ())), pr...  79.8 us
    psum x1, blocking collectives, on_device(): scale_gradient = lax.psum(scale_terms, ('dp', 'tensor')) / replicas  41 us
    dot_general x1, matrix products, on_device(): lax.dot_general(dpre, w_in, (((1,), (1,)), ((), ())), preferred_element_t...  39.6 us
    dot_general x1, matrix products, contract_rows(): lax.dot_general(left, right, (((0,), (0,)), ((), ())), preferred_element_...  29 us
    dot_general x1, matrix products, on_device(): pre = jnp.dot(full, w_in, preferred_element_type=jnp.float32)  26.8 us
  transfers between devices with their start and end apart: 3, of which 3 were waited for; matrix products, arithmetic and copies ran while one was open for 7% of the time, Pallas kernels for 0%

commit v1 on v0

v1 whole, which is shorter than its diff:
```python
import functools

import jax
import jax.numpy as jnp
from jax import lax
from jax.experimental import pallas as pl
from jax.experimental.pallas import tpu as pltpu
from jax.sharding import PartitionSpec as P

MESH = pl.DeviceIdType.MESH
STAGES = 2


def contract_rows(left, right):
    return lax.dot_general(
        left, right, (((0,), (0,)), ((), ())), preferred_element_type=jnp.float32
    )


def gelu_slope(v):
    c = 0.7978845608028654
    vv = v * v
    th = jnp.tanh(c * v * (1.0 + 0.044715 * vv))
    return 0.5 * (1.0 + th) + 0.5 * v * (1.0 - th * th) * (c * (1.0 + 0.134145 * vv))


def kernel(
    n_t, n_h, J, c,
    nrm, w, ga, ng, gd, gn,
    w_v, ag, part, rr, dp,
    ld_w, ld_ga, ld_n,
    ag_recv, ag_send_r, ag_send_l,
    xn_send, xn_recv, xd_send, xd_recv,
    rs_recv_r, rs_recv_l, rs_send_r, rs_send_l,
    cn, cd, cg,
):
    t = lax.axis_index("tensor")
    d = lax.axis_index("dp")
    hi, core = d // 2, lax.rem(d, 2)
    D, F = w_v.shape
    W = D // n_h
    last = n_t - 1

    def rows(s):
        return pl.ds(pl.multiple_of(s * c, c), c)

    def peer(p):
        return lax.rem(hi + p, n_h)

    def came_from(p):
        return lax.rem(hi - p + n_h, n_h)

    def step(right):
        return {"tensor": lax.rem(t + 1, n_t) if right else lax.rem(t + last, n_t)}

    def ag_copy(j, s, right):
        block = ag.at[j, rows(s), :]
        sems = ag_send_r if right else ag_send_l
        return pltpu.make_async_remote_copy(
            block, block, sems.at[j, s], ag_recv.at[j, s],
            device_id=step(right), device_id_type=MESH)

    def rs_copy(j, s, right):
        slot = s + 1 if right else s
        send, recv = (rs_send_r, rs_recv_l) if right else (rs_send_l, rs_recv_r)
        return pltpu.make_async_remote_copy(
            part.at[j, rows(s), :], rr.at[j, rows(slot), :], send.at[j, s], recv.at[j, s],
            device_id=step(right), device_id_type=MESH)

    def xn_copy(j, s, p, whose):
        cols = pl.ds(pl.multiple_of(peer(p) * W, W), W)
        return pltpu.make_async_remote_copy(
            ag.at[j, rows(s), cols], ng.at[whose, j, rows(s), :],
            xn_send.at[j, s, p], xn_recv.at[j, s, p],
            device_id={"dp": peer(p) * 2 + core}, device_id_type=MESH)

    def xd_copy(j, p, whose):
        return pltpu.make_async_remote_copy(
            dp.at[j], gd.at[whose, j], xd_send.at[j, p], xd_recv.at[j, p],
            device_id={"dp": peer(p) * 2 + core}, device_id_type=MESH)

    def own_cols(j):
        return pltpu.make_async_copy(
            ag.at[j, :, pl.ds(pl.multiple_of(hi * W, W), W)], ng.at[hi, j], cn.at[j])

    def own_dpre(j):
        return pltpu.make_async_copy(dp.at[j], gd.at[hi, j], cd.at[j])

    pieces = ld_w.shape[0]
    depth = D // pieces

    def w_copy(i):
        r = pl.ds(i * depth, depth)
        return pltpu.make_async_copy(w.at[r, :], w_v.at[r, :], ld_w.at[i])

    def n_copy(j):
        return pltpu.make_async_copy(nrm.at[j], ag.at[j, rows(t), :], ld_n.at[j])

    def ga_copy(j, s):
        return pltpu.make_async_copy(ga.at[s, j], dp.at[j, pl.ds(s * c, c), :], ld_ga.at[j, s])

    for j in range(J):
        n_copy(j).start()
    barrier = pltpu.get_barrier_semaphore()
    for right in (True, False):
        @pl.when(t < last if right else t > 0)
        def _():
            pl.semaphore_signal(barrier, inc=1, device_id=step(right), device_id_type=MESH)
    for p in range(1, n_h):
        pl.semaphore_signal(barrier, inc=1, device_id={"dp": peer(p) * 2 + core}, device_id_type=MESH)
    pl.semaphore_wait(barrier, n_h - 1 + jnp.minimum(t, 1) + jnp.minimum(last - t, 1))
    for j in range(J):
        n_copy(j).wait()

    def send_own(j, right):
        @pl.when(t < last if right else t > 0)
        def _():
            ag_copy(j, t, right).start()

    def spread(j, s):
        for p in range(1, n_h):
            xn_copy(j, s, p, hi).start()

    send_own(0, True)
    send_own(0, False)
    for i in range(pieces):
        w_copy(i).start()
    for j in range(J):
        for s in range(n_t):
            ga_copy(j, s).start()
    for j in range(J):
        spread(j, t)

    def next_own(j, k):
        if j + 1 < J:
            @pl.when(k == t)
            def _():
                send_own(j + 1, True)

            @pl.when(k == last - t)
            def _():
                send_own(j + 1, False)

    def ag_round(j, k):
        next_own(j, k)

        @pl.when(k < t)
        def _():
            s = t - 1 - k
            ag_copy(j, s, True).wait_recv()

            @pl.when(t < last)
            def _():
                ag_copy(j, s, True).start()
            spread(j, s)

        @pl.when(k < last - t)
        def _():
            s = t + 1 + k
            ag_copy(j, s, False).wait_recv()

            @pl.when(t > 0)
            def _():
                ag_copy(j, s, False).start()
            spread(j, s)

    def make_dpre(j):
        ft = 512 if F % 512 == 0 else 256

        def tile(i, _):
            cols = pl.ds(pl.multiple_of(i * ft, ft), ft)
            pre = jnp.dot(ag[j], w_v[:, cols], preferred_element_type=jnp.float32)
            g = dp[j, :, cols].astype(jnp.float32)
            dp[j, :, cols] = (g * gelu_slope(pre)).astype(jnp.bfloat16)
            return 0
        lax.fori_loop(0, F // ft, tile, 0)
        for p in range(1, n_h):
            xd_copy(j, p, hi).start()
        own_dpre(j).start()

    def make_parts(j):
        dt = 256

        def tile(i, _):
            cols = pl.ds(pl.multiple_of(i * dt, dt), dt)
            part[j, :, cols] = lax.dot_general(
                dp[j], w_v[cols, :], (((1,), (1,)), ((), ())),
                preferred_element_type=jnp.float32).astype(jnp.bfloat16)
            return 0
        lax.fori_loop(0, D // dt, tile, 0)

    def add(j, s, slot):
        def some(i, _):
            a = pl.ds(pl.multiple_of(s * c + i * 16, 16), 16)
            b = pl.ds(pl.multiple_of(slot * c + i * 16, 16), 16)
            part[j, a, :] = (
                part[j, a, :].astype(jnp.float32) + rr[j, b, :].astype(jnp.float32)
            ).astype(jnp.bfloat16)
            return 0
        lax.fori_loop(0, c // 16, some, 0)

    def rs_round(j, r):
        @pl.when(r <= t)
        def _():
            @pl.when(t < last)
            def _():
                rs_copy(j, r, False).wait_recv()
                add(j, r, r)

            @pl.when(r < t)
            def _():
                rs_copy(j, r, False).start()

        @pl.when(last - r >= t)
        def _():
            s = last - r

            @pl.when(t > 0)
            def _():
                rs_copy(j, s, True).wait_recv()
                add(j, s, s + 1)

            @pl.when(s > t)
            def _():
                rs_copy(j, s, True).start()

    def loop(lo, hi_, body):
        def run(k, _):
            body(k)
            return 0
        lax.fori_loop(lo, hi_, run, 0)

    def done_out(j):
        return pltpu.make_async_copy(part.at[j, rows(t), :], gn.at[j], cg.at[j])

    loop(0, last, lambda k: ag_round(0, k))
    next_own(0, last)
    for i in range(pieces):
        w_copy(i).wait()
    for j in range(J):
        for s in range(n_t):
            ga_copy(j, s).wait()

    for j in range(J):
        own_cols(j).start()
        make_dpre(j)
        more = j + 1 < J
        if more:
            ag_round(j + 1, 0)
        else:
            if j > 0:
                rs_round(j - 1, last)
                done_out(j - 1).start()
        make_parts(j)
        if more:
            def both(r, j=j):
                rs_round(j, r)
                ag_round(j + 1, r + 1)
            loop(0, last - 1, both)
            rs_round(j, last - 1)
            next_own(j + 1, last)
        else:
            loop(0, n_t, lambda r: rs_round(j, r))
            done_out(j).start()

    for j in range(J):
        own_cols(j).wait()
        own_dpre(j).wait()
        done_out(j).wait()
        for p in range(1, n_h):
            xd_copy(j, p, came_from(p)).wait_recv()
            xd_copy(j, p, hi).wait_send()

        def finish(s, j=j):
            for p in range(1, n_h):
                xn_copy(j, s, p, came_from(p)).wait_recv()
                xn_copy(j, s, p, hi).wait_send()

            @pl.when((s <= t) & (t < last))
            def _():
                ag_copy(j, s, True).wait_send()

            @pl.when((s >= t) & (t > 0))
            def _():
                ag_copy(j, s, False).wait_send()

            @pl.when(s > t)
            def _():
                rs_copy(j, s, True).wait_send()

            @pl.when(s < t)
            def _():
                rs_copy(j, s, False).wait_send()
        loop(0, n_t, finish)


def exchange(normed, w_in, grad_act):
    n_t, n_d = lax.axis_size("tensor"), lax.axis_size("dp")
    n_h = n_d // 2
    J = STAGES
    local, D = normed.shape
    F = w_in.shape[1]
    c = local // J
    tok = n_t * c
    bf = jnp.bfloat16
    dma = pltpu.SemaphoreType.DMA
    hbm = pl.BlockSpec(memory_space=pl.ANY)
    flops = 4 * J * tok * D * F
    return pl.pallas_call(
        functools.partial(kernel, n_t, n_h, J, c),
        out_shape=(
            jax.ShapeDtypeStruct((n_h, J, tok, D // n_h), bf),
            jax.ShapeDtypeStruct((n_h, J, tok, F), bf),
            jax.ShapeDtypeStruct((J, c, D), bf),
        ),
        in_specs=[hbm] * 3,
        out_specs=(hbm, hbm, hbm),
        scratch_shapes=[
            pltpu.VMEM((D, F), bf),
            pltpu.VMEM((J, tok, D), bf),
            pltpu.VMEM((J, tok, D), bf),
            pltpu.VMEM((J, tok + c, D), bf),
            pltpu.VMEM((J, tok, F), bf),
            dma((8,)), dma((J, n_t)), dma((J,)),
            dma((J, n_t)), dma((J, n_t)), dma((J, n_t)),
            dma((J, n_t, n_h)), dma((J, n_t, n_h)), dma((J, n_h)), dma((J, n_h)),
            dma((J, n_t)), dma((J, n_t)), dma((J, n_t)), dma((J, n_t)),
            dma((J,)), dma((J,)), dma((J,)),
        ],
        cost_estimate=pl.CostEstimate(
            flops=flops, bytes_accessed=2 * D * F, transcendentals=J * tok * F),
        compiler_params=pltpu.CompilerParams(
            collective_id=0, has_side_effects=True, vmem_limit_bytes=64 * 1024 * 1024 - 131072),
    )(normed.reshape(J, c, D), w_in, grad_act.reshape(n_t, J, c, F))


def on_device(inputs, gain, w_in, grad_act, residual_gradient):
    values = inputs.astype(jnp.float32)
    centered_input = values - jnp.mean(values, axis=1, keepdims=True)
    inverse_deviation = lax.rsqrt(
        jnp.mean(centered_input * centered_input, axis=1, keepdims=True) + 1e-06
    )
    standardized_input = centered_input * inverse_deviation
    normed_output = (standardized_input * gain).astype(jnp.bfloat16)
    replicas = lax.axis_size("dp")
    ng, gd, gn = exchange(normed_output, w_in, grad_act)

    normed_gradient = gn.reshape(inputs.shape).astype(jnp.float32)
    scale_terms = jnp.sum(normed_gradient * standardized_input, axis=0)
    scale_gradient = lax.psum(scale_terms, ("dp", "tensor")) / replicas
    scaled_gradient = normed_gradient * gain
    first_average = jnp.mean(scaled_gradient, axis=1, keepdims=True)
    second_average = jnp.mean(scaled_gradient * standardized_input, axis=1, keepdims=True)
    block_input_gradient = (
        residual_gradient.astype(jnp.float32)
        + inverse_deviation
        * (scaled_gradient - first_average - standardized_input * second_average)
    ).astype(jnp.bfloat16)

    core = lax.rem(lax.axis_index("dp"), 2)
    cols = ng.reshape(-1, ng.shape[-1])
    dpre = gd.reshape(-1, gd.shape[-1])
    half = cols.shape[1] // 2
    theirs = lax.dynamic_slice_in_dim(cols, (1 - core) * half, half, 1)
    mine = lax.dynamic_slice_in_dim(cols, core * half, half, 1)
    sent = contract_rows(theirs, dpre).astype(jnp.bfloat16)
    got = lax.ppermute(sent, "dp", [(i, i ^ 1) for i in range(replicas)])
    grad_w = (contract_rows(mine, dpre) + got.astype(jnp.float32)) / replicas
    return (block_input_gradient, grad_w, scale_gradient)


def solution(mesh):
    return jax.shard_map(
        on_device,
        mesh=mesh,
        in_specs=(
            P(("dp", "tensor"), None),
            P(),
            P(None, "tensor"),
            P("dp", "tensor"),
            P(("dp", "tensor"), None),
        ),
        out_specs=(P(("dp", "tensor"), None), P("dp", "tensor"), P()),
        check_vma=False,
    )
```

time: 551 us -> 407 us (0.74)
  waiting for transfers between devices: 379 us -> 0.01 us
  Pallas kernels: 0 us -> 282 us
  matrix products: 95.4 us -> 31.5 us
  blocking collectives: 41 us -> 81.2 us
  between operations: 13.8 us -> 0.71 us
  other arithmetic: 22.1 us -> 12.1 us
    pallas_call x0 -> x1, Pallas kernels: none -> 282 us  [exchange(): pl.pallas_call(functools.partial(kernel, n_t, n_h, J, c), out_shape=(jax....]
    reduce_scatter x2 -> x0, waiting for transfers between devices: 260 us -> none  [the longest x1 181 us: on_device(): lax.psum_scatter(term.astype(jnp.bfloat16), 'dp', scatter_dimension=0, ti...]
    all_gather x1 -> x0, waiting for transfers between devices: 118 us -> none  [on_device(): full = lax.all_gather(normed_output, 'tensor', axis=0, tiled=True)]
    dot_general x2 -> x0, matrix products: 66.3 us -> none  [the longest x1 39.6 us: on_device(): lax.dot_general(dpre, w_in, (((1,), (1,)), ((), ())), preferred_element_t...]
    psum x1, blocking collectives: 41 us -> 81.2 us  [on_device(): scale_gradient = lax.psum(scale_terms, ('dp', 'tensor')) / replicas]
    div x1, other arithmetic: 7.33 us -> 0.01 us  [on_device(): first_average = jnp.mean(scaled_gradient, axis=1, keepdims=True)]
    dot_general x1 -> x2, matrix products: 29 us -> 31.5 us  [contract_rows(): lax.dot_general(left, right, (((0,), (0,)), ((), ())), preferred_element_...]
  transfers between devices with their start and end apart: 3 -> 1, of which waited for: 3 -> 0; matrix products, arithmetic and copies ran while one was open for 7% -> 2% of each run, Pallas kernels for 0% -> 0%
where the time goes in v1:
time: 407 us
  Pallas kernels  282 us (69%)
  blocking collectives  81.2 us (20%)
  matrix products  31.5 us (8%)
  other arithmetic  12.1 us (3%)
    pallas_call x1, Pallas kernels, exchange(): pl.pallas_call(functools.partial(kernel, n_t, n_h, J, c), out_shape=(jax....  282 us
    psum x1, blocking collectives, on_device(): scale_gradient = lax.psum(scale_terms, ('dp', 'tensor')) / replicas  81.2 us
    dot_general x2, matrix products, contract_rows(): lax.dot_general(left, right, (((0,), (0,)), ((), ())), preferred_element_...  31.5 us
  transfers between devices with their start and end apart: 1, of which 0 were waited for; matrix products, arithmetic and copies ran while one was open for 2% of the time, Pallas kernels for 0%

profile of v1, /device:TPU:0, one launch (start us, length us, event | category | flops | bytes accessed | tf_op | source)
XLA Modules:
  0.0 407.1 jit_solution(7725270277652001487)
XLA Ops:
  0.6 0.0 copy-start
  0.6 0.0 copy-start.3
  0.7 1.8 convert_reduce_fusion
  2.5 2.0 fusion.13
  4.5 0.0 copy-done
  4.5 0.0 copy-done.3
  4.5 1.7 fusion.6
  6.2 281.5 %shard_map.76 = (bf16[4,2,256,1536]{3,2,1,0:T(8,128)(2,1)}, bf16[4,2,256,3072]{3,2,1,0:T(8,128)(2,1)}, bf16[2,64,6144]{2,1,0:T(8,128)(2,1)}) custom-call(bf16[2,64,6144]{2,1,0:T(8,128)(2,1)} %bitcast.15, bf16[6144,3072]{1,0:T(8,128)(2,1)} %w.1, bf16[4,2,64,3072]{3,2,1,0:T(8,128)(2,1)} %bitcast.16), custom_call_target="tpu_custom_call" | custom-call | flops 38654705664 | bytes 37748736 | tf_op jit(solution)/shard_map/pallas_call | solution.py:309
  287.7 0.0 copy-start.2
  287.7 0.0 copy-start.1
  287.7 15.5 %convolution_convert_fusion = bf16[768,3072]{1,0:T(8,128)(2,1)} fusion(bf16[2048,3072]{1,0:T(8,128)(2,1)} %bitcast.17, bf16[2048,1536]{1,0:T(8,128)(2,1)} %bitcast.19, s32[]{:T(128)S(6)} %select_n.7), kind=kOutput, calls=%fused_computation.1 | convolution fusion | flops 9666035712 | bytes 20447236 | tf_op jit(solution)/shard_map/dot_general | solution.py:15
  303.2 0.0 collective-permute-start
  303.2 0.0 copy-done.2
  303.2 0.4 fusion.15
  303.6 0.1 div.29
  303.7 0.0 copy-done.1
  303.7 1.3 fusion.12
  305.0 81.2 %psum.7 = f32[6144]{0:T(1024)S(1)} all-reduce(f32[6144]{0:T(1024)S(1)} %get-tuple-element.9), channel_id=1, replica_groups=mesh['dp'=8,'tensor'=4] {'dp','tensor'}, use_global_device_ids=true, to_apply=%region_5.0 | all-reduce | flops 6144 | bytes 49152 | tf_op jit(solution)/shard_map/psum | solution.py:350
  386.2 0.6 broadcast_multiply_fusion
  386.8 0.0 copy-start.4
  386.8 4.3 %fusion.11 = bf16[128,6144]{1,0:T(8,128)(2,1)} fusion(bf16[128,6144]{1,0:T(8,128)(2,1)S(1)} %copy-done.1, bf16[2,64,6144]{2,1,0:T(8,128)(2,1)S(1)} %copy-done.2, bf16[128,6144]{1,0:T(8,128)(2,1)} %param.9, f32[128]{0:T(128)S(1)} %broadcast_multiply_fusion.2, f32[128]{0:T(128)S(1)} %div.29, f32[6144]{0:T(1024)S(1)} %copy-done.3, f32[128]{0:T(128)S(1)} %add_rsqrt_fusion, ...), kind=kLoop, calls=%fused_computation.15 | loop fusion | flops 9437184 | bytes 6318080 | tf_op jit(solution)/shard_map/convert_element_type | solution.py:358
  391.1 0.0 collective-permute-done
  391.1 0.0 copy-done.4
  391.1 16.0 %add_multiply_fusion = f32[768,3072]{1,0:T(8,128)} fusion(bf16[768,3072]{1,0:T(8,128)(2,1)} %collective-permute-done, bf16[2048,3072]{1,0:T(8,128)(2,1)} %bitcast.18, bf16[2048,1536]{1,0:T(8,128)(2,1)S(1)} %bitcast.20, s32[]{:T(128)S(6)} %select_n.6), kind=kOutput, calls=%fused_computation | convolution fusion | flops 9670754304 | bytes 29884420 | tf_op jit(solution)/shard_map/dot_general | solution.py:15
  (4 shorter events, 0.0 us)
Async XLA Ops:
  0.6 3.8 copy-start
  0.6 3.8 copy-start.3
  287.7 15.5 %copy-start.2 = (bf16[2,64,6144]{2,1,0:T(8,128)(2,1)S(1)}, bf16[2,64,6144]{2,1,0:T(8,128)(2,1)}, u32[]{:S(2)}) copy-start(bf16[2,64,6144]{2,1,0:T(8,128)(2,1)} %get-tuple-element.6) | copy-start | bytes 4718596
  287.7 16.0 %copy-start.1 = (bf16[128,6144]{1,0:T(8,128)(2,1)S(1)}, bf16[128,6144]{1,0:T(8,128)(2,1)}, u32[]{:S(2)}) copy-start(bf16[128,6144]{1,0:T(8,128)(2,1)} %param.5) | copy-start | bytes 4718596
  303.2 87.9 %collective-permute-start = (bf16[768,3072]{1,0:T(8,128)(2,1)}, bf16[768,3072]{1,0:T(8,128)(2,1)}, u32[]{:S(2)}, u32[]{:S(2)}) collective-permute-start(bf16[768,3072]{1,0:T(8,128)(2,1)} %convolution_convert_fusion), channel_id=1, source_target_pairs={{0,4},{4,0},{8,12},{12,8},{16,20},{20,16},{24,28},{28,24},{1,5},{5... | collective-permute-start | bytes 14155784 | tf_op jit(solution)/shard_map/ppermute | solution.py:367
  386.8 4.3 %copy-start.4 = (bf16[4,2,256,1536]{3,2,1,0:T(8,128)(2,1)S(1)}, bf16[4,2,256,1536]{3,2,1,0:T(8,128)(2,1)}, u32[]{:S(2)}) copy-start(bf16[4,2,256,1536]{3,2,1,0:T(8,128)(2,1)} %get-tuple-element.7) | copy-start | bytes 18874372
